TPU v7x, 512 devices: a whole 4x8x8 slice. The times are simulated.
512 devices in a mesh: lon: 32 (over z_hi, x, core), lat: 16 (over y, z_lo).
Axes of the slice: x: 4, y: 8, z: 8 (z_hi: 4, z_lo: 2; z = z_hi * 2 + z_lo), core: 2. Of those that a mesh axis runs over, the one named last changes fastest.
Arguments:
- fields: bfloat16 [96, 128, 8192], P(None, 'lat', 'lon'), may hold values from -6 to 6
- land_mask: int32 [128, 8192], P('lat', 'lon'), may hold values from 0 to 1, as said below
- dw_kernel: float32 [96, 7, 7], replicated, may hold values from -0.875 to 0.875
- gain: float32 [96], replicated, may hold values from 0.1 to 1.9
- w_in: bfloat16 [96, 192], replicated, may hold values from -0.625 to 0.625
- b_in: float32 [192], replicated, may hold values from -3 to 3
- w_out: bfloat16 [192, 96], replicated, may hold values from -0.4375 to 0.4375
- cotangent: bfloat16 [96, 128, 8192], P(None, 'lat', 'lon'), may hold values from -6 to 6
Outputs:
- output: bfloat16 [96, 128, 8192], P(None, 'lat', 'lon')
- input_grad: bfloat16 [96, 128, 8192], P(None, 'lat', 'lon')
- kernel_grad: float32 [96, 7, 7], replicated
- gain_grad: float32 [96], replicated
- w_in_grad: float32 [96, 192], replicated
- b_in_grad: float32 [192], replicated
- w_out_grad: float32 [192, 96], replicated
Inputs may be any that keep to these rules, and one draw needn't show every extreme that they name: `land_mask`: 1 marks a sea cell and 0 a land cell.
All inputs are finite; a program needn't handle non-finite values.
Results may differ from a plain program's by a relative error of at most 0.009.
Values may be sent and summed in bfloat16 or wider, within the bound.
No kernel may reach another device: no remote copies, remote signals or barrier semaphores. Data moves between devices by JAX's collectives and lax.ppermute only.
A program may use at most 192 MiB of HBM per device.

v0:
```python
import jax
import jax.numpy as jnp
from jax import lax
from jax.sharding import PartitionSpec as P


def from_partner(block, axis, stride):
    count = lax.axis_size(axis)
    route = []
    for low in range(count):
        high = low | 1 << stride
        if high != low and high < count:
            route += [(low, high), (high, low)]
    return lax.ppermute(block, axis, route)


def extended(shard, sides, width, wrap):
    for axis, dim in sides:
        size, length = (lax.axis_size(axis), shard.shape[dim])
        up = [(i, (i + 1) % size) for i in range(size if wrap else size - 1)]
        down = [(j, i) for i, j in up]
        last = lax.slice_in_dim(shard, length - width, length, axis=dim)
        first = lax.slice_in_dim(shard, 0, width, axis=dim)
        before = lax.ppermute(last, axis, up)
        after = lax.ppermute(first, axis, down)
        shard = jnp.concatenate([before, shard, after], axis=dim)
    return shard


def mirror_forward(values):
    steps_count = lax.axis_size("lon").bit_length() - 1
    for bit_pos in range(steps_count):
        values = from_partner(values, "lon", bit_pos)
    return values[:, ::-1, ::-1]


def mirror_backward(values):
    steps_count = lax.axis_size("lon").bit_length() - 1
    for bit_pos in range(steps_count):
        values = from_partner(values.astype(jnp.bfloat16), "lon", bit_pos).astype(values.dtype)
    return values[:, ::-1, ::-1]


def convolve(padded, kernel, tile_rows, tile_cols):
    summed = jnp.zeros((padded.shape[0], tile_rows, tile_cols), jnp.float32)
    for row_off in range(7):
        for col_off in range(7):
            window = padded[:, row_off : row_off + tile_rows, col_off : col_off + tile_cols].astype(
                jnp.float32
            )
            summed = summed + kernel[:, row_off, col_off][:, None, None] * window
    return summed


def spread_back(conv_grad, kernel):
    channels, tile_rows, tile_cols = conv_grad.shape
    bordered = jnp.pad(conv_grad, ((0, 0), (6, 6), (6, 6)))
    summed = jnp.zeros((channels, tile_rows + 6, tile_cols + 6), jnp.float32)
    for row_off in range(7):
        for col_off in range(7):
            window = bordered[
                :, 6 - row_off : 12 - row_off + tile_rows, 6 - col_off : 12 - col_off + tile_cols
            ]
            summed = summed + kernel[:, row_off, col_off][:, None, None] * window
    return summed


def kernel_terms(conv_grad, padded):
    channels, tile_rows, tile_cols = conv_grad.shape
    terms = []
    for row_off in range(7):
        for col_off in range(7):
            window = padded[:, row_off : row_off + tile_rows, col_off : col_off + tile_cols].astype(
                jnp.float32
            )
            terms.append(jnp.sum(conv_grad * window, axis=(1, 2)))
    return jnp.stack(terms, axis=1).reshape(channels, 7, 7)


def shards(fields, land_mask, dw_kernel, gain, w_in, b_in, w_out, cotangent):
    channels, tile_rows, tile_cols = fields.shape
    sea_mask = land_mask.astype(jnp.bfloat16)[None]
    masked = fields * sea_mask
    back_sea = cotangent * sea_mask
    lat_pos = lax.axis_index("lat")
    is_bottom = lat_pos == 0
    is_top = lat_pos == lax.axis_size("lat") - 1
    padded = extended(masked, (("lon", 2), ("lat", 1)), 3, True)
    folded = mirror_forward(padded[:, tile_rows : tile_rows + 3, :])
    south = jnp.where(is_bottom, jnp.zeros_like(padded[:, :3, :]), padded[:, :3, :])
    north = jnp.where(is_top, folded, padded[:, tile_rows + 3 :, :])
    padded = jnp.concatenate([south, padded[:, 3 : tile_rows + 3, :], north], axis=1)
    conv_out = convolve(padded, dw_kernel, tile_rows, tile_cols)
    centred = conv_out - jnp.mean(conv_out, axis=0, keepdims=True)
    inv_std = lax.rsqrt(jnp.mean(centred * centred, axis=0, keepdims=True) + 1e-06)
    normed = centred * inv_std
    scaled = (normed * gain[:, None, None]).astype(jnp.bfloat16)
    hidden_pre = (
        jnp.einsum("ch,cxy->hxy", w_in, scaled, preferred_element_type=jnp.float32)
        + b_in[:, None, None]
    )
    activated, gelu_pull = jax.vjp(jax.nn.gelu, hidden_pre)
    activated = activated.astype(jnp.bfloat16)
    mixed = jnp.einsum("hc,hxy->cxy", w_out, activated, preferred_element_type=jnp.float32)
    centre = padded[:, 3 : tile_rows + 3, 3 : tile_cols + 3].astype(jnp.float32)
    output = (sea_mask * (centre + mixed)).astype(jnp.bfloat16)
    w_out_part = jnp.einsum("hxy,cxy->hc", activated, back_sea, preferred_element_type=jnp.float32)
    act_grad = jnp.einsum("hc,cxy->hxy", w_out, back_sea, preferred_element_type=jnp.float32)
    pre_grad = gelu_pull(act_grad)[0].astype(jnp.bfloat16)
    output, w_out_part, pre_grad, scaled, normed, inv_std = (
        output,
        w_out_part,
        pre_grad,
        scaled,
        normed,
        inv_std,
    )
    b_part = jnp.sum(pre_grad.astype(jnp.float32), axis=(1, 2))
    w_in_part = jnp.einsum("cxy,hxy->ch", scaled, pre_grad, preferred_element_type=jnp.float32)
    scaled_grad = jnp.einsum("ch,hxy->cxy", w_in, pre_grad, preferred_element_type=jnp.float32)
    gain_part = jnp.sum(scaled_grad * normed, axis=(1, 2))
    norm_grad = scaled_grad * gain[:, None, None]
    conv_grad = inv_std * (
        norm_grad
        - jnp.mean(norm_grad, axis=0, keepdims=True)
        - normed * jnp.mean(norm_grad * normed, axis=0, keepdims=True)
    )
    kernel_part = kernel_terms(conv_grad, padded)
    ext_grad = spread_back(conv_grad, dw_kernel)
    kernel_part, gain_part, w_in_part, b_part, ext_grad = (
        kernel_part,
        gain_part,
        w_in_part,
        b_part,
        ext_grad,
    )
    kernel_sum, gain_sum, w_in_sum, b_sum, w_out_sum = lax.psum(
        (kernel_part, gain_part, w_in_part, b_part, w_out_part), ("lon", "lat")
    )
    returned = mirror_backward(ext_grad[:, tile_rows + 3 :, :])
    ext_grad = ext_grad.at[:, tile_rows : tile_rows + 3, :].add(
        jnp.where(is_top, returned, jnp.zeros_like(returned))
    )
    rims = jnp.concatenate([ext_grad[:, :3, :], ext_grad[:, tile_rows + 3 :, :]], axis=1)
    got_rows = extended(rims.astype(jnp.bfloat16), (("lat", 1),), 3, False).astype(rims.dtype)
    inner = ext_grad[:, 3 : tile_rows + 3, :]
    inner = inner.at[:, :3, :].add(got_rows[:, :3, :])
    inner = inner.at[:, tile_rows - 3 :, :].add(got_rows[:, 9:, :])
    sides = jnp.concatenate([inner[:, :, :3], inner[:, :, tile_cols + 3 :]], axis=2)
    sides = jnp.transpose(sides, (2, 0, 1)).reshape(6, channels * tile_rows)
    got_cols = extended(sides, (("lon", 0),), 3, True)
    from_left = jnp.transpose(got_cols[:3].reshape(3, channels, tile_rows), (1, 2, 0))
    from_right = jnp.transpose(got_cols[9:].reshape(3, channels, tile_rows), (1, 2, 0))
    core = inner[:, :, 3 : tile_cols + 3]
    core = core.at[:, :, :3].add(from_left)
    core = core.at[:, :, tile_cols - 3 :].add(from_right)
    input_grad = (sea_mask * (core + back_sea.astype(jnp.float32))).astype(jnp.bfloat16)
    scale_factor = float(tile_rows * tile_cols * lax.axis_size("lat") * lax.axis_size("lon")) ** (
        -0.5
    )
    return (
        output,
        input_grad,
        kernel_sum * scale_factor,
        gain_sum * scale_factor,
        w_in_sum * scale_factor,
        b_sum * scale_factor,
        w_out_sum * scale_factor,
    )


def solution(mesh):
    return jax.shard_map(
        shards,
        mesh=mesh,
        in_specs=(
            P(None, "lat", "lon"),
            P("lat", "lon"),
            P(),
            P(),
            P(),
            P(),
            P(),
            P(None, "lat", "lon"),
        ),
        out_specs=(P(None, "lat", "lon"), P(None, "lat", "lon"), P(), P(), P(), P(), P()),
        check_vma=False,
    )
```

profile of v0, /device:TPU:7, one launch (start us, length us, event | category | flops | bytes accessed | tf_op | source)
XLA Modules:
  0.0 450.5 jit_solution(8596428200641927452)
XLA Ops:
  9.1 6.3 %collective-permute-start = (bf16[96,8,3]{2,0,1:T(8,128)(2,1)S(1)}, bf16[96,8,3]{2,0,1:T(8,128)(2,1)S(1)}, u32[]{:S(2)}, u32[]{:S(2)}) collective-permute-start(bf16[96,8,3]{2,0,1:T(8,128)(2,1)S(1)} %get-tuple-element.168), channel_id=1, source_target_pairs={{0,16},{16,32},{32,48},{48,64},{64,80},{80,96},{96,112},{112,128},... | collective-permute-start | bytes 13832 | tf_op jit(solution)/shard_map/ppermute | solution.py:24
  18.0 9.6 %collective-permute-done.1 = bf16[96,8,3]{2,0,1:T(8,128)(2,1)S(1)} collective-permute-done((bf16[96,8,3]{2,0,1:T(8,128)(2,1)S(1)}, bf16[96,8,3]{2,0,1:T(8,128)(2,1)S(1)}, u32[]{:S(2)}, u32[]{:S(2)}) %collective-permute-start.1) | collective-permute-done | bytes 4640 | tf_op jit(solution)/shard_map/ppermute | solution.py:25
  33.4 6.7 %collective-permute-done.4 = bf16[96,3,262]{2,0,1:T(8,128)(2,1)S(1)} collective-permute-done((bf16[96,3,262]{2,0,1:T(8,128)(2,1)S(1)}, bf16[96,3,262]{2,0,1:T(8,128)(2,1)S(1)}, u32[]{:S(2)}, u32[]{:S(2)}) %collective-permute-start.4) | collective-permute-done | bytes 150944 | tf_op jit(solution)/shard_map/ppermute | solution.py:14
  40.1 4.1 collective-permute-start.5
  49.4 8.1 %collective-permute-start.6 = (bf16[96,3,262]{2,0,1:T(8,128)(2,1)S(1)}, bf16[96,3,262]{2,0,1:T(8,128)(2,1)S(1)}, u32[]{:S(2)}, u32[]{:S(2)}) collective-permute-start(bf16[96,3,262]{2,0,1:T(8,128)(2,1)S(1)} %collective-permute-done.5), channel_id=1, source_target_pairs={{0,128},{128,0},{16,144},{144,16},{32,160},{160,32},{48,176},{176,... | collective-permute-start | bytes 452744 | tf_op jit(solution)/shard_map/ppermute | solution.py:14
  58.1 5.2 %collective-permute-start.8 = (bf16[96,3,262]{2,0,1:T(8,128)(2,1)S(1)}, bf16[96,3,262]{2,0,1:T(8,128)(2,1)S(1)}, u32[]{:S(2)}, u32[]{:S(2)}) collective-permute-start(bf16[96,3,262]{2,0,1:T(8,128)(2,1)S(1)} %get-tuple-element.166), channel_id=1, source_target_pairs={{1,0},{2,1},{3,2},{4,3},{5,4},{6,5},{7,6},{8,7},{9,8},{10,9},{11,1... | collective-permute-start | bytes 452744 | tf_op jit(solution)/shard_map/ppermute | solution.py:25
  63.3 4.0 collective-permute-done.6
  67.3 5.6 %collective-permute-start.7 = (bf16[96,3,262]{2,0,1:T(8,128)(2,1)S(1)}, bf16[96,3,262]{2,0,1:T(8,128)(2,1)S(1)}, u32[]{:S(2)}, u32[]{:S(2)}) collective-permute-start(bf16[96,3,262]{2,0,1:T(8,128)(2,1)S(1)} %collective-permute-done.6), channel_id=1, source_target_pairs={{0,256},{256,0},{16,272},{272,16},{32,288},{288,32},{48,304},{304,... | collective-permute-start | bytes 452744 | tf_op jit(solution)/shard_map/ppermute | solution.py:14
  73.0 9.9 %collective-permute-done.7 = bf16[96,3,262]{2,0,1:T(8,128)(2,1)S(1)} collective-permute-done((bf16[96,3,262]{2,0,1:T(8,128)(2,1)S(1)}, bf16[96,3,262]{2,0,1:T(8,128)(2,1)S(1)}, u32[]{:S(2)}, u32[]{:S(2)}) %collective-permute-start.7) | collective-permute-done | bytes 150944 | tf_op jit(solution)/shard_map/ppermute | solution.py:14
  84.8 8.7 %fusion.223 = (f32[8,256]{1,0:T(8,128)S(1)}, f32[96,8,256]{2,0,1:T(8,128)S(1)}) fusion(bf16[96,11,262]{2,0,1:T(8,128)(2,1)S(1)} %get-tuple-element.165, f32[96]{0:T(128)} %get-tuple-element.217, f32[96]{0:T(128)} %get-tuple-element.218, f32[96]{0:T(128)S(1)} %get-tuple-element.171, f32[96]{0:T(128)S(1)} %get-tuple-element.172, ...), kind=kLoop, calls=%fused_computation.474 | loop fusion | flops 32438272 | bytes 17730944 | tf_op jit(solution)/shard_map/reduce_sum | solution.py:94
  106.0 17.7 %fusion.93 = f32[96,14,262]{2,0,1:T(8,128)S(1)} fusion(f32[96,8,256]{2,0,1:T(8,128)S(1)} %get-tuple-element.155, f32[96]{0:T(128)} %get-tuple-element.217, f32[96]{0:T(128)} %get-tuple-element.218, f32[96]{0:T(128)S(1)} %get-tuple-element.171, f32[96]{0:T(128)S(1)} %get-tuple-element.172, f32[96]{0:T(128)S(1)} %get-tuple-element.173, ...), kind=kLoop, calls=%fused_computation.144 | loop fusion | flops 34156416 | bytes 2213760 | tf_op jit(solution)/shard_map/add | solution.py:64
  128.1 4.3 stack.199
  132.5 4.3 collective-permute-start.9
  143.5 103.7 %all-reduce.1 = (f32[96,7,7]{0,2,1:T(8,128)S(1)}, f32[96]{0:T(128)S(1)}, f32[192]{0:T(256)S(1)}) all-reduce(f32[96,7,7]{0,2,1:T(8,128)S(1)} %reshape.198, f32[96]{0:T(128)S(1)} %copy-done.87, f32[192]{0:T(256)S(1)} %copy-done.97), channel_id=1, replica_groups=mesh['lon'=32,'lat'=16] {'lon','lat'}, use_global_device_ids=true, to_apply=%region_53.54 | all-reduce | flops 4992 | bytes 39936 | tf_op jit(solution)/shard_map/psum | solution.py:137
  247.2 4.5 %collective-permute-start.11 = (bf16[96,3,262]{2,0,1:T(8,128)(2,1)S(1)}, bf16[96,3,262]{2,0,1:T(8,128)(2,1)S(1)}, u32[]{:S(2)}, u32[]{:S(2)}) collective-permute-start(bf16[96,3,262]{2,0,1:T(8,128)(2,1)S(1)} %collective-permute-done.10), channel_id=1, source_target_pairs={{0,64},{64,0},{16,80},{80,16},{32,96},{96,32},{48,112},{112,48},{1... | collective-permute-start | bytes 452744 | tf_op jit(solution)/shard_map/ppermute | solution.py:14
  252.3 4.4 collective-permute-done.11
  260.2 10.0 %collective-permute-done.12 = bf16[96,3,262]{2,0,1:T(8,128)(2,1)S(1)} collective-permute-done((bf16[96,3,262]{2,0,1:T(8,128)(2,1)S(1)}, bf16[96,3,262]{2,0,1:T(8,128)(2,1)S(1)}, u32[]{:S(2)}, u32[]{:S(2)}) %collective-permute-start.12) | collective-permute-done | bytes 150944 | tf_op jit(solution)/shard_map/ppermute | solution.py:14
  270.2 4.3 collective-permute-start.13
  275.0 12.5 %collective-permute-done.13 = bf16[96,3,262]{2,0,1:T(8,128)(2,1)S(1)} collective-permute-done((bf16[96,3,262]{2,0,1:T(8,128)(2,1)S(1)}, bf16[96,3,262]{2,0,1:T(8,128)(2,1)S(1)}, u32[]{:S(2)}, u32[]{:S(2)}) %collective-permute-start.13) | collective-permute-done | bytes 150944 | tf_op jit(solution)/shard_map/ppermute | solution.py:14
  292.6 120.1 %all-reduce.5.cloned.1.call-done = (f32[96,192]{1,0:T(8,128)}, f32[192,96]{1,0:T(8,128)}) async-done(((f32[96,192]{1,0:T(8,128)}, f32[192,96]{1,0:T(8,128)}), (f32[96,192]{1,0:T(8,128)}, f32[192,96]{1,0:T(8,128)})) %all-reduce.5.cloned.1.call-update) | async-done | bytes 147472 | tf_op jit(solution)/shard_map/psum | solution.py:137
  417.2 3.7 collective-permute-start.16
  425.0 5.2 %collective-permute-done.17 = f32[3,768]{1,0:T(4,128)S(1)} collective-permute-done((f32[3,768]{1,0:T(4,128)S(1)}, f32[3,768]{1,0:T(4,128)S(1)}, u32[]{:S(2)}, u32[]{:S(2)}) %collective-permute-start.17) | collective-permute-done | bytes 9248 | tf_op jit(solution)/shard_map/ppermute | solution.py:25
  431.0 6.0 %scatter-add.21 = f32[96,8,256]{2,0,1:T(8,128)S(1)} dynamic-update-slice(f32[96,8,256]{2,0,1:T(8,128)S(1)} %slice.989, f32[96,8,3]{2,0,1:T(8,128)S(1)} %slice_add_fusion.3, s32[]{:T(128)} %constant.159.clone.1, s32[]{:T(128)} %constant.159.clone.1, s32[]{:T(128)} %constant.159.clone.1) | dynamic-update-slice | bytes 18436 | tf_op jit(solution)/shard_map/scatter-add | solution.py:155
  437.2 5.3 %scatter-add.24 = f32[96,8,256]{2,0,1:T(8,128)S(1)} dynamic-update-slice(f32[96,8,256]{2,0,1:T(8,128)S(1)} %scatter-add.21, f32[96,8,3]{2,0,1:T(8,128)S(1)} %slice_add_fusion.2, s32[]{:T(128)} %constant.159.clone.1, s32[]{:T(128)} %constant.159.clone.1, s32[]{:T(128)} %constant.173.clone.1) | dynamic-update-slice | bytes 18436 | tf_op jit(solution)/shard_map/scatter-add | solution.py:156
  (278 shorter events, 60.7 us)
Async XLA Ops:
  7.2 86.5 %copy-start = (bf16[96,192]{1,0:T(8,128)(2,1)S(1)}, bf16[96,192]{1,0:T(8,128)(2,1)}, u32[]{:S(2)}) copy-start(bf16[96,192]{1,0:T(8,128)(2,1)} %param.22) | copy-start | bytes 110596
  7.2 405.5 %all-reduce.5.cloned.1.call-start = ((), (), s32[]{:S(2)}) async-start(), calls=%async_computation | async-start | bytes 393216 | tf_op jit(solution)/shard_map/psum | solution.py:137
  9.1 8.9 %collective-permute-start = (bf16[96,8,3]{2,0,1:T(8,128)(2,1)S(1)}, bf16[96,8,3]{2,0,1:T(8,128)(2,1)S(1)}, u32[]{:S(2)}, u32[]{:S(2)}) collective-permute-start(bf16[96,8,3]{2,0,1:T(8,128)(2,1)S(1)} %get-tuple-element.168), channel_id=1, source_target_pairs={{0,16},{16,32},{32,48},{48,64},{64,80},{80,96},{96,112},{112,128},... | collective-permute-start | bytes 13832 | tf_op jit(solution)/shard_map/ppermute | solution.py:24
  15.4 12.2 %collective-permute-start.1 = (bf16[96,8,3]{2,0,1:T(8,128)(2,1)S(1)}, bf16[96,8,3]{2,0,1:T(8,128)(2,1)S(1)}, u32[]{:S(2)}, u32[]{:S(2)}) collective-permute-start(bf16[96,8,3]{2,0,1:T(8,128)(2,1)S(1)} %get-tuple-element.169), channel_id=1, source_target_pairs={{16,0},{32,16},{48,32},{64,48},{80,64},{96,80},{112,96},{128,112},... | collective-permute-start | bytes 13832 | tf_op jit(solution)/shard_map/ppermute | solution.py:25
  27.6 56.8 %copy-start.1 = (bf16[96,8,3]{2,0,1:T(8,128)(2,1)}, bf16[96,8,3]{2,0,1:T(8,128)(2,1)S(1)}, u32[]{:S(2)}) copy-start(bf16[96,8,3]{2,0,1:T(8,128)(2,1)S(1)} %collective-permute-done.1) | copy-start | bytes 13828
  27.9 3.4 collective-permute-start.3
  31.3 8.8 %collective-permute-start.4 = (bf16[96,3,262]{2,0,1:T(8,128)(2,1)S(1)}, bf16[96,3,262]{2,0,1:T(8,128)(2,1)S(1)}, u32[]{:S(2)}, u32[]{:S(2)}) collective-permute-start(bf16[96,3,262]{2,0,1:T(8,128)(2,1)S(1)} %collective-permute-done.3), channel_id=1, source_target_pairs={{0,32},{32,0},{16,48},{48,16},{64,96},{96,64},{80,112},{112,80},{1... | collective-permute-start | bytes 452744 | tf_op jit(solution)/shard_map/ppermute | solution.py:14
  33.2 51.2 %copy-start.11 = (f32[96]{0:T(128)}, f32[96]{0:T(128)S(1)}, u32[]{:S(2)}) copy-start(f32[96]{0:T(128)S(1)} %get-tuple-element.176) | copy-start | bytes 1156
  33.2 51.2 %copy-start.13 = (f32[96]{0:T(128)}, f32[96]{0:T(128)S(1)}, u32[]{:S(2)}) copy-start(f32[96]{0:T(128)S(1)} %get-tuple-element.177) | copy-start | bytes 1156
  33.2 51.2 %copy-start.15 = (f32[96]{0:T(128)}, f32[96]{0:T(128)S(1)}, u32[]{:S(2)}) copy-start(f32[96]{0:T(128)S(1)} %get-tuple-element.178) | copy-start | bytes 1156
  40.1 9.4 %collective-permute-start.5 = (bf16[96,3,262]{2,0,1:T(8,128)(2,1)S(1)}, bf16[96,3,262]{2,0,1:T(8,128)(2,1)S(1)}, u32[]{:S(2)}, u32[]{:S(2)}) collective-permute-start(bf16[96,3,262]{2,0,1:T(8,128)(2,1)S(1)} %collective-permute-done.4), channel_id=1, source_target_pairs={{0,64},{64,0},{16,80},{80,16},{32,96},{96,32},{48,112},{112,48},{1... | collective-permute-start | bytes 452744 | tf_op jit(solution)/shard_map/ppermute | solution.py:14
  44.4 28.5 %collective-permute-start.2 = (bf16[96,3,262]{2,0,1:T(8,128)(2,1)S(1)}, bf16[96,3,262]{2,0,1:T(8,128)(2,1)S(1)}, u32[]{:S(2)}, u32[]{:S(2)}) collective-permute-start(bf16[96,3,262]{2,0,1:T(8,128)(2,1)S(1)} %get-tuple-element.167), channel_id=1, source_target_pairs={{0,1},{1,2},{2,3},{3,4},{4,5},{5,6},{6,7},{7,8},{8,9},{9,10},{10,1... | collective-permute-start | bytes 452744 | tf_op jit(solution)/shard_map/ppermute | solution.py:24
  49.4 17.9 %collective-permute-start.6 = (bf16[96,3,262]{2,0,1:T(8,128)(2,1)S(1)}, bf16[96,3,262]{2,0,1:T(8,128)(2,1)S(1)}, u32[]{:S(2)}, u32[]{:S(2)}) collective-permute-start(bf16[96,3,262]{2,0,1:T(8,128)(2,1)S(1)} %collective-permute-done.5), channel_id=1, source_target_pairs={{0,128},{128,0},{16,144},{144,16},{32,160},{160,32},{48,176},{176,... | collective-permute-start | bytes 452744 | tf_op jit(solution)/shard_map/ppermute | solution.py:14
  58.1 25.6 %collective-permute-start.8 = (bf16[96,3,262]{2,0,1:T(8,128)(2,1)S(1)}, bf16[96,3,262]{2,0,1:T(8,128)(2,1)S(1)}, u32[]{:S(2)}, u32[]{:S(2)}) collective-permute-start(bf16[96,3,262]{2,0,1:T(8,128)(2,1)S(1)} %get-tuple-element.166), channel_id=1, source_target_pairs={{1,0},{2,1},{3,2},{4,3},{5,4},{6,5},{7,6},{8,7},{9,8},{10,9},{11,1... | collective-permute-start | bytes 452744 | tf_op jit(solution)/shard_map/ppermute | solution.py:25
  67.3 15.5 %collective-permute-start.7 = (bf16[96,3,262]{2,0,1:T(8,128)(2,1)S(1)}, bf16[96,3,262]{2,0,1:T(8,128)(2,1)S(1)}, u32[]{:S(2)}, u32[]{:S(2)}) collective-permute-start(bf16[96,3,262]{2,0,1:T(8,128)(2,1)S(1)} %collective-permute-done.6), channel_id=1, source_target_pairs={{0,256},{256,0},{16,272},{272,16},{32,288},{288,32},{48,304},{304,... | collective-permute-start | bytes 452744 | tf_op jit(solution)/shard_map/ppermute | solution.py:14
  132.5 7.1 %collective-permute-start.9 = (bf16[96,3,262]{2,0,1:T(8,128)(2,1)S(1)}, bf16[96,3,262]{2,0,1:T(8,128)(2,1)}, u32[]{:S(2)}, u32[]{:S(2)}) collective-permute-start(bf16[96,3,262]{2,0,1:T(8,128)(2,1)S(1)} %slice.1622), channel_id=1, source_target_pairs={{0,16},{16,0},{32,48},{48,32},{64,80},{80,64},{96,112},{112,96},{1... | collective-permute-start | bytes 452744 | tf_op jit(solution)/shard_map/ppermute | solution.py:14
  139.6 107.6 %collective-permute-start.10 = (bf16[96,3,262]{2,0,1:T(8,128)(2,1)}, bf16[96,3,262]{2,0,1:T(8,128)(2,1)S(1)}, u32[]{:S(2)}, u32[]{:S(2)}) collective-permute-start(bf16[96,3,262]{2,0,1:T(8,128)(2,1)} %collective-permute-done.9), channel_id=1, source_target_pairs={{0,32},{32,0},{16,48},{48,16},{64,96},{96,64},{80,112},{112,80},{1... | collective-permute-start | bytes 452744 | tf_op jit(solution)/shard_map/ppermute | solution.py:14
  247.2 9.5 %collective-permute-start.11 = (bf16[96,3,262]{2,0,1:T(8,128)(2,1)S(1)}, bf16[96,3,262]{2,0,1:T(8,128)(2,1)S(1)}, u32[]{:S(2)}, u32[]{:S(2)}) collective-permute-start(bf16[96,3,262]{2,0,1:T(8,128)(2,1)S(1)} %collective-permute-done.10), channel_id=1, source_target_pairs={{0,64},{64,0},{16,80},{80,16},{32,96},{96,32},{48,112},{112,48},{1... | collective-permute-start | bytes 452744 | tf_op jit(solution)/shard_map/ppermute | solution.py:14
  256.6 13.6 %collective-permute-start.12 = (bf16[96,3,262]{2,0,1:T(8,128)(2,1)S(1)}, bf16[96,3,262]{2,0,1:T(8,128)(2,1)S(1)}, u32[]{:S(2)}, u32[]{:S(2)}) collective-permute-start(bf16[96,3,262]{2,0,1:T(8,128)(2,1)S(1)} %collective-permute-done.11), channel_id=1, source_target_pairs={{0,128},{128,0},{16,144},{144,16},{32,160},{160,32},{48,176},{176,... | collective-permute-start | bytes 452744 | tf_op jit(solution)/shard_map/ppermute | solution.py:14
  270.2 17.3 %collective-permute-start.13 = (bf16[96,3,262]{2,0,1:T(8,128)(2,1)S(1)}, bf16[96,3,262]{2,0,1:T(8,128)(2,1)S(1)}, u32[]{:S(2)}, u32[]{:S(2)}) collective-permute-start(bf16[96,3,262]{2,0,1:T(8,128)(2,1)S(1)} %collective-permute-done.12), channel_id=1, source_target_pairs={{0,256},{256,0},{16,272},{272,16},{32,288},{288,32},{48,304},{304,... | collective-permute-start | bytes 452744 | tf_op jit(solution)/shard_map/ppermute | solution.py:14
  289.4 125.0 %collective-permute-start.14 = (bf16[96,3,262]{2,0,1:T(8,128)(2,1)S(1)}, bf16[96,3,262]{2,0,1:T(8,128)(2,1)}, u32[]{:S(2)}, u32[]{:S(2)}) collective-permute-start(bf16[96,3,262]{2,0,1:T(8,128)(2,1)S(1)} %get-tuple-element.162), channel_id=1, source_target_pairs={{0,1},{1,2},{2,3},{3,4},{4,5},{5,6},{6,7},{7,8},{8,9},{9,10},{10,1... | collective-permute-start | bytes 452744 | tf_op jit(solution)/shard_map/ppermute | solution.py:24
  291.4 123.0 %collective-permute-start.15 = (bf16[96,3,262]{2,0,1:T(8,128)(2,1)}, bf16[96,3,262]{2,0,1:T(8,128)(2,1)}, u32[]{:S(2)}, u32[]{:S(2)}) collective-permute-start(bf16[96,3,262]{2,0,1:T(8,128)(2,1)} %get-tuple-element.163), channel_id=1, source_target_pairs={{1,0},{2,1},{3,2},{4,3},{5,4},{6,5},{7,6},{8,7},{9,8},{10,9},{11,1... | collective-permute-start | bytes 452744 | tf_op jit(solution)/shard_map/ppermute | solution.py:25
  417.2 6.8 %collective-permute-start.16 = (f32[3,768]{1,0:T(4,128)S(1)}, f32[3,768]{1,0:T(4,128)S(1)}, u32[]{:S(2)}, u32[]{:S(2)}) collective-permute-start(f32[3,768]{1,0:T(4,128)S(1)} %slice.926), channel_id=1, source_target_pairs={{0,16},{16,32},{32,48},{48,64},{64,80},{80,96},{96,112},{112,128},... | collective-permute-start | bytes 27656 | tf_op jit(solution)/shard_map/ppermute | solution.py:24
  422.1 8.2 %collective-permute-start.17 = (f32[3,768]{1,0:T(4,128)S(1)}, f32[3,768]{1,0:T(4,128)S(1)}, u32[]{:S(2)}, u32[]{:S(2)}) collective-permute-start(f32[3,768]{1,0:T(4,128)S(1)} %slice.929), channel_id=1, source_target_pairs={{16,0},{32,16},{48,32},{64,48},{80,64},{96,80},{112,96},{128,112},... | collective-permute-start | bytes 27656 | tf_op jit(solution)/shard_map/ppermute | solution.py:25
  (94 other events, 1737.3 us)
Sparse Core Ops, SparseCore 0:
  143.6 269.0 all-reduce.4
where the time goes:
time: 451 us
  waiting for transfers between devices  188 us (42%)
  blocking collectives  104 us (23%)
  starting transfers between devices  64.7 us (14%)
  other arithmetic  46.5 us (10%)
  local copies, waits for them, and re-layouts  24.3 us (5%)
  between operations  15.9 us (4%)
  matrix products  7.92 us (2%)
    psum x1, waiting for transfers between devices, shards(): lax.psum((kernel_part, gain_part, w_in_part, b_part, w_out_part), ('lon',...  120 us
    psum x1, blocking collectives, shards(): lax.psum((kernel_part, gain_part, w_in_part, b_part, w_out_part), ('lon',...  104 us
    ppermute x10, waiting for transfers between devices, from_partner(): return lax.ppermute(block, axis, route)  51.9 us
    ppermute x10, starting transfers between devices, from_partner(): return lax.ppermute(block, axis, route)  40.5 us
    add x1, other arithmetic, spread_back(): summed = summed + kernel[:, row_off, col_off][:, None, None] * window  17.7 us
    ppermute x4, waiting for transfers between devices, extended(): after = lax.ppermute(first, axis, down)  14.8 us
    ppermute x4, starting transfers between devices, extended(): before = lax.ppermute(last, axis, up)  13.9 us
    reduce_sum x4, other arithmetic, kernel_terms(): terms.append(jnp.sum(conv_grad * window, axis=(1, 2)))  10.5 us
  transfers between devices with their start and end apart: 19, of which 12 were waited for; matrix products, arithmetic and copies ran while one was open for 3% of the time, Pallas kernels for 0%

commit v1 on v0

--- a/solution.py
+++ b/solution.py
@@ -135,7 +135,7 @@
         ext_grad,
     )
     kernel_sum, gain_sum, w_in_sum, b_sum, w_out_sum = lax.psum(
-        (kernel_part, gain_part, w_in_part, b_part, w_out_part), ("lon", "lat")
+        lax.psum((kernel_part, gain_part, w_in_part, b_part, w_out_part), "lon"), "lat"
     )
     returned = mirror_backward(ext_grad[:, tile_rows + 3 :, :])
     ext_grad = ext_grad.at[:, tile_rows : tile_rows + 3, :].add(

time: 451 us -> 607 us (1.35)
  blocking collectives: 104 us -> 170 us
  waiting for transfers between devices: 188 us -> 244 us
  starting transfers between devices: 64.7 us -> 97.2 us
    psum x1 -> x2, waiting for transfers between devices: 120 us -> 198 us  [the longest x1 136 us: shards(): lax.psum(lax.psum((kernel_part, gain_part, w_in_part, b_part, w_out_part)...]
    psum x1 -> x2, blocking collectives: 104 us -> 170 us  [the longest x1 118 us: shards(): lax.psum((kernel_part, gain_part, w_in_part, b_part, w_out_part), 'lon')]
    ppermute x10, waiting for transfers between devices: 51.9 us -> 30.7 us  [from_partner(): return lax.ppermute(block, axis, route)]
    ppermute x10, starting transfers between devices: 40.5 us -> 59.8 us  [from_partner(): return lax.ppermute(block, axis, route)]
    ppermute x4, starting transfers between devices: 13.9 us -> 27.1 us  [extended(): before = lax.ppermute(last, axis, up)]
  transfers between devices with their start and end apart: 19 -> 20, of which waited for: 12 -> 12; matrix products, arithmetic and copies ran while one was open for 3% -> 2% of each run, Pallas kernels for 0% -> 0%
where the time goes in v1:
time: 607 us; the launch traced here: 606 us
  waiting for transfers between devices  244 us (40%)
  blocking collectives  170 us (28%)
  starting transfers between devices  97.2 us (16%)
  other arithmetic  46.5 us (8%)
  local copies, waits for them, and re-layouts  24.3 us (4%)
  between operations  15.9 us (3%)
  matrix products  7.92 us (1%)
    psum x1, waiting for transfers between devices, shards(): lax.psum(lax.psum((kernel_part, gain_part, w_in_part, b_part, w_out_part)...  136 us
    psum x1, blocking collectives, shards(): lax.psum((kernel_part, gain_part, w_in_part, b_part, w_out_part), 'lon')  118 us
    psum x1, waiting for transfers between devices, shards(): lax.psum((kernel_part, gain_part, w_in_part, b_part, w_out_part), 'lon')  61.8 us
    ppermute x10, starting transfers between devices, from_partner(): return lax.ppermute(block, axis, route)  59.8 us
    psum x1, blocking collectives, shards(): lax.psum(lax.psum((kernel_part, gain_part, w_in_part, b_part, w_out_part)...  51.6 us
    ppermute x10, waiting for transfers between devices, from_partner(): return lax.ppermute(block, axis, route)  30.7 us
    ppermute x4, starting transfers between devices, extended(): before = lax.ppermute(last, axis, up)  27.1 us
    add x1, other arithmetic, spread_back(): summed = summed + kernel[:, row_off, col_off][:, None, None] * window  17.7 us
  transfers between devices with their start and end apart: 20, of which 12 were waited for; matrix products, arithmetic and copies ran while one was open for 2% of the time, Pallas kernels for 0%

profile of v1, /device:TPU:7, one launch (start us, length us, event | category | flops | bytes accessed | tf_op | source)
XLA Modules:
  0.0 605.7 jit_solution(9326804059304566500)
XLA Ops:
  9.1 6.3 %collective-permute-start = (bf16[96,8,3]{2,0,1:T(8,128)(2,1)S(1)}, bf16[96,8,3]{2,0,1:T(8,128)(2,1)S(1)}, u32[]{:S(2)}, u32[]{:S(2)}) collective-permute-start(bf16[96,8,3]{2,0,1:T(8,128)(2,1)S(1)} %get-tuple-element.173), channel_id=1, source_target_pairs={{0,16},{16,32},{32,48},{48,64},{64,80},{80,96},{96,112},{112,128},... | collective-permute-start | bytes 13832 | tf_op jit(solution)/shard_map/ppermute | solution.py:24
  18.0 9.6 %collective-permute-done.1 = bf16[96,8,3]{2,0,1:T(8,128)(2,1)S(1)} collective-permute-done((bf16[96,8,3]{2,0,1:T(8,128)(2,1)S(1)}, bf16[96,8,3]{2,0,1:T(8,128)(2,1)S(1)}, u32[]{:S(2)}, u32[]{:S(2)}) %collective-permute-start.1) | collective-permute-done | bytes 4640 | tf_op jit(solution)/shard_map/ppermute | solution.py:25
  33.4 6.7 %collective-permute-done.4 = bf16[96,3,262]{2,0,1:T(8,128)(2,1)S(1)} collective-permute-done((bf16[96,3,262]{2,0,1:T(8,128)(2,1)S(1)}, bf16[96,3,262]{2,0,1:T(8,128)(2,1)S(1)}, u32[]{:S(2)}, u32[]{:S(2)}) %collective-permute-start.4) | collective-permute-done | bytes 150944 | tf_op jit(solution)/shard_map/ppermute | solution.py:14
  40.1 4.1 collective-permute-start.5
  49.4 8.1 %collective-permute-start.6 = (bf16[96,3,262]{2,0,1:T(8,128)(2,1)S(1)}, bf16[96,3,262]{2,0,1:T(8,128)(2,1)S(1)}, u32[]{:S(2)}, u32[]{:S(2)}) collective-permute-start(bf16[96,3,262]{2,0,1:T(8,128)(2,1)S(1)} %collective-permute-done.5), channel_id=1, source_target_pairs={{0,128},{128,0},{16,144},{144,16},{32,160},{160,32},{48,176},{176,... | collective-permute-start | bytes 452744 | tf_op jit(solution)/shard_map/ppermute | solution.py:14
  58.1 5.2 collective-permute-start.8
  63.3 4.0 collective-permute-done.6
  67.3 5.6 collective-permute-start.7
  73.0 9.9 %collective-permute-done.7 = bf16[96,3,262]{2,0,1:T(8,128)(2,1)S(1)} collective-permute-done((bf16[96,3,262]{2,0,1:T(8,128)(2,1)S(1)}, bf16[96,3,262]{2,0,1:T(8,128)(2,1)S(1)}, u32[]{:S(2)}, u32[]{:S(2)}) %collective-permute-start.7) | collective-permute-done | bytes 150944 | tf_op jit(solution)/shard_map/ppermute | solution.py:14
  84.8 8.7 %fusion.223 = (f32[8,256]{1,0:T(8,128)S(1)}, f32[96,8,256]{2,0,1:T(8,128)S(1)}) fusion(bf16[96,11,262]{2,0,1:T(8,128)(2,1)S(1)} %get-tuple-element.170, f32[96]{0:T(128)} %get-tuple-element.222, f32[96]{0:T(128)} %get-tuple-element.223, f32[96]{0:T(128)S(1)} %get-tuple-element.176, f32[96]{0:T(128)S(1)} %get-tuple-element.177, ...), kind=kLoop, calls=%fused_computation.474 | loop fusion | flops 32438272 | bytes 17730944 | tf_op jit(solution)/shard_map/reduce_sum | solution.py:94
  97.4 3.5 fusion.206
  106.0 17.7 %fusion.93 = f32[96,14,262]{2,0,1:T(8,128)S(1)} fusion(f32[96,8,256]{2,0,1:T(8,128)S(1)} %get-tuple-element.160, f32[96]{0:T(128)} %get-tuple-element.222, f32[96]{0:T(128)} %get-tuple-element.223, f32[96]{0:T(128)S(1)} %get-tuple-element.176, f32[96]{0:T(128)S(1)} %get-tuple-element.177, f32[96]{0:T(128)S(1)} %get-tuple-element.178, ...), kind=kLoop, calls=%fused_computation.144 | loop fusion | flops 34156416 | bytes 2213760 | tf_op jit(solution)/shard_map/add | solution.py:64
  128.1 4.3 stack.199
  132.5 4.3 collective-permute-start.9
  143.5 118.3 %all-reduce.1 = (f32[96,7,7]{0,2,1:T(8,128)S(1)}, f32[96]{0:T(128)S(1)}, f32[192]{0:T(256)S(1)}) all-reduce(f32[96,7,7]{0,2,1:T(8,128)S(1)} %reshape.198, f32[96]{0:T(128)S(1)} %copy-done.87, f32[192]{0:T(256)S(1)} %copy-done.97), channel_id=1, replica_groups=mesh['lon'=32,'lat'=16] {'lon'}, use_global_device_ids=true, to_apply=%region_53.54 | all-reduce | flops 4992 | bytes 39936 | tf_op jit(solution)/shard_map/psum | solution.py:138
  261.8 51.6 %all-reduce.3 = (f32[96,7,7]{0,2,1:T(8,128)S(1)}, f32[96]{0:T(128)S(1)}, f32[192]{0:T(256)S(1)}) all-reduce(f32[96,7,7]{0,2,1:T(8,128)S(1)} %get-tuple-element.150, f32[96]{0:T(128)S(1)} %get-tuple-element.151, f32[192]{0:T(256)S(1)} %get-tuple-element.152), channel_id=1, replica_groups=mesh['lon'=32,'lat'=16] {'lat'}, use_global_device_ids=true, to_apply=%region_54.55 | all-reduce | flops 4992 | bytes 39936 | tf_op jit(solution)/shard_map/psum | solution.py:137
  313.4 13.8 %collective-permute-start.11 = (bf16[96,3,262]{2,0,1:T(8,128)(2,1)S(1)}, bf16[96,3,262]{2,0,1:T(8,128)(2,1)S(1)}, u32[]{:S(2)}, u32[]{:S(2)}) collective-permute-start(bf16[96,3,262]{2,0,1:T(8,128)(2,1)S(1)} %collective-permute-done.10), channel_id=1, source_target_pairs={{0,64},{64,0},{16,80},{80,16},{32,96},{96,32},{48,112},{112,48},{1... | collective-permute-start | bytes 452744 | tf_op jit(solution)/shard_map/ppermute | solution.py:14
  330.5 14.3 %collective-permute-start.12 = (bf16[96,3,262]{2,0,1:T(8,128)(2,1)S(1)}, bf16[96,3,262]{2,0,1:T(8,128)(2,1)S(1)}, u32[]{:S(2)}, u32[]{:S(2)}) collective-permute-start(bf16[96,3,262]{2,0,1:T(8,128)(2,1)S(1)} %collective-permute-done.11), channel_id=1, source_target_pairs={{0,128},{128,0},{16,144},{144,16},{32,160},{160,32},{48,176},{176,... | collective-permute-start | bytes 452744 | tf_op jit(solution)/shard_map/ppermute | solution.py:14
  351.7 61.8 %all-reduce.8.cloned.1.call-done = (f32[96,192]{1,0:T(8,128)}, f32[192,96]{1,0:T(8,128)}) async-done(((f32[96,192]{1,0:T(8,128)}, f32[192,96]{1,0:T(8,128)}), (f32[96,192]{1,0:T(8,128)}, f32[192,96]{1,0:T(8,128)})) %all-reduce.8.cloned.1.call-update) | async-done | bytes 147472 | tf_op jit(solution)/shard_map/psum | solution.py:138
  419.8 136.0 %all-reduce.10.cloned.1.call-done = (f32[96,192]{1,0:T(8,128)}, f32[192,96]{1,0:T(8,128)}) async-done(((f32[96,192]{1,0:T(8,128)}, f32[192,96]{1,0:T(8,128)}), (f32[96,192]{1,0:T(8,128)}, f32[192,96]{1,0:T(8,128)})) %all-reduce.10.cloned.1.call-update) | async-done | bytes 147472 | tf_op jit(solution)/shard_map/psum | solution.py:137
  560.4 15.8 %collective-permute-start.16 = (f32[3,768]{1,0:T(4,128)S(1)}, f32[3,768]{1,0:T(4,128)S(1)}, u32[]{:S(2)}, u32[]{:S(2)}) collective-permute-start(f32[3,768]{1,0:T(4,128)S(1)} %slice.926), channel_id=1, source_target_pairs={{0,16},{16,32},{32,48},{48,64},{64,80},{80,96},{96,112},{112,128},... | collective-permute-start | bytes 27656 | tf_op jit(solution)/shard_map/ppermute | solution.py:24
  580.3 5.1 collective-permute-done.17
  586.2 6.0 scatter-add.21
  592.4 5.3 scatter-add.24
  (282 shorter events, 63.8 us)
Async XLA Ops:
  7.2 86.5 %copy-start = (bf16[96,192]{1,0:T(8,128)(2,1)S(1)}, bf16[96,192]{1,0:T(8,128)(2,1)}, u32[]{:S(2)}) copy-start(bf16[96,192]{1,0:T(8,128)(2,1)} %param.22) | copy-start | bytes 110596
  7.2 406.4 %all-reduce.8.cloned.1.call-start = ((), (), s32[]{:S(2)}) async-start(), calls=%async_computation | async-start | bytes 393216 | tf_op jit(solution)/shard_map/psum | solution.py:138
  9.1 8.9 %collective-permute-start = (bf16[96,8,3]{2,0,1:T(8,128)(2,1)S(1)}, bf16[96,8,3]{2,0,1:T(8,128)(2,1)S(1)}, u32[]{:S(2)}, u32[]{:S(2)}) collective-permute-start(bf16[96,8,3]{2,0,1:T(8,128)(2,1)S(1)} %get-tuple-element.173), channel_id=1, source_target_pairs={{0,16},{16,32},{32,48},{48,64},{64,80},{80,96},{96,112},{112,128},... | collective-permute-start | bytes 13832 | tf_op jit(solution)/shard_map/ppermute | solution.py:24
  15.4 12.2 %collective-permute-start.1 = (bf16[96,8,3]{2,0,1:T(8,128)(2,1)S(1)}, bf16[96,8,3]{2,0,1:T(8,128)(2,1)S(1)}, u32[]{:S(2)}, u32[]{:S(2)}) collective-permute-start(bf16[96,8,3]{2,0,1:T(8,128)(2,1)S(1)} %get-tuple-element.174), channel_id=1, source_target_pairs={{16,0},{32,16},{48,32},{64,48},{80,64},{96,80},{112,96},{128,112},... | collective-permute-start | bytes 13832 | tf_op jit(solution)/shard_map/ppermute | solution.py:25
  27.6 56.8 %copy-start.1 = (bf16[96,8,3]{2,0,1:T(8,128)(2,1)}, bf16[96,8,3]{2,0,1:T(8,128)(2,1)S(1)}, u32[]{:S(2)}) copy-start(bf16[96,8,3]{2,0,1:T(8,128)(2,1)S(1)} %collective-permute-done.1) | copy-start | bytes 13828
  27.9 3.4 collective-permute-start.3
  31.3 8.8 %collective-permute-start.4 = (bf16[96,3,262]{2,0,1:T(8,128)(2,1)S(1)}, bf16[96,3,262]{2,0,1:T(8,128)(2,1)S(1)}, u32[]{:S(2)}, u32[]{:S(2)}) collective-permute-start(bf16[96,3,262]{2,0,1:T(8,128)(2,1)S(1)} %collective-permute-done.3), channel_id=1, source_target_pairs={{0,32},{32,0},{16,48},{48,16},{64,96},{96,64},{80,112},{112,80},{1... | collective-permute-start | bytes 452744 | tf_op jit(solution)/shard_map/ppermute | solution.py:14
  33.2 51.2 %copy-start.11 = (f32[96]{0:T(128)}, f32[96]{0:T(128)S(1)}, u32[]{:S(2)}) copy-start(f32[96]{0:T(128)S(1)} %get-tuple-element.181) | copy-start | bytes 1156
  33.2 51.2 %copy-start.13 = (f32[96]{0:T(128)}, f32[96]{0:T(128)S(1)}, u32[]{:S(2)}) copy-start(f32[96]{0:T(128)S(1)} %get-tuple-element.182) | copy-start | bytes 1156
  40.1 9.4 %collective-permute-start.5 = (bf16[96,3,262]{2,0,1:T(8,128)(2,1)S(1)}, bf16[96,3,262]{2,0,1:T(8,128)(2,1)S(1)}, u32[]{:S(2)}, u32[]{:S(2)}) collective-permute-start(bf16[96,3,262]{2,0,1:T(8,128)(2,1)S(1)} %collective-permute-done.4), channel_id=1, source_target_pairs={{0,64},{64,0},{16,80},{80,16},{32,96},{96,32},{48,112},{112,48},{1... | collective-permute-start | bytes 452744 | tf_op jit(solution)/shard_map/ppermute | solution.py:14
  44.4 28.5 %collective-permute-start.2 = (bf16[96,3,262]{2,0,1:T(8,128)(2,1)S(1)}, bf16[96,3,262]{2,0,1:T(8,128)(2,1)S(1)}, u32[]{:S(2)}, u32[]{:S(2)}) collective-permute-start(bf16[96,3,262]{2,0,1:T(8,128)(2,1)S(1)} %get-tuple-element.172), channel_id=1, source_target_pairs={{0,1},{1,2},{2,3},{3,4},{4,5},{5,6},{6,7},{7,8},{8,9},{9,10},{10,1... | collective-permute-start | bytes 452744 | tf_op jit(solution)/shard_map/ppermute | solution.py:24
  49.4 17.9 %collective-permute-start.6 = (bf16[96,3,262]{2,0,1:T(8,128)(2,1)S(1)}, bf16[96,3,262]{2,0,1:T(8,128)(2,1)S(1)}, u32[]{:S(2)}, u32[]{:S(2)}) collective-permute-start(bf16[96,3,262]{2,0,1:T(8,128)(2,1)S(1)} %collective-permute-done.5), channel_id=1, source_target_pairs={{0,128},{128,0},{16,144},{144,16},{32,160},{160,32},{48,176},{176,... | collective-permute-start | bytes 452744 | tf_op jit(solution)/shard_map/ppermute | solution.py:14
  58.1 25.6 %collective-permute-start.8 = (bf16[96,3,262]{2,0,1:T(8,128)(2,1)S(1)}, bf16[96,3,262]{2,0,1:T(8,128)(2,1)S(1)}, u32[]{:S(2)}, u32[]{:S(2)}) collective-permute-start(bf16[96,3,262]{2,0,1:T(8,128)(2,1)S(1)} %get-tuple-element.171), channel_id=1, source_target_pairs={{1,0},{2,1},{3,2},{4,3},{5,4},{6,5},{7,6},{8,7},{9,8},{10,9},{11,1... | collective-permute-start | bytes 452744 | tf_op jit(solution)/shard_map/ppermute | solution.py:25
  67.3 15.5 %collective-permute-start.7 = (bf16[96,3,262]{2,0,1:T(8,128)(2,1)S(1)}, bf16[96,3,262]{2,0,1:T(8,128)(2,1)S(1)}, u32[]{:S(2)}, u32[]{:S(2)}) collective-permute-start(bf16[96,3,262]{2,0,1:T(8,128)(2,1)S(1)} %collective-permute-done.6), channel_id=1, source_target_pairs={{0,256},{256,0},{16,272},{272,16},{32,288},{288,32},{48,304},{304,... | collective-permute-start | bytes 452744 | tf_op jit(solution)/shard_map/ppermute | solution.py:14
  132.5 7.1 %collective-permute-start.9 = (bf16[96,3,262]{2,0,1:T(8,128)(2,1)S(1)}, bf16[96,3,262]{2,0,1:T(8,128)(2,1)}, u32[]{:S(2)}, u32[]{:S(2)}) collective-permute-start(bf16[96,3,262]{2,0,1:T(8,128)(2,1)S(1)} %slice.1622), channel_id=1, source_target_pairs={{0,16},{16,0},{32,48},{48,32},{64,80},{80,64},{96,112},{112,96},{1... | collective-permute-start | bytes 452744 | tf_op jit(solution)/shard_map/ppermute | solution.py:14
  139.6 173.8 %collective-permute-start.10 = (bf16[96,3,262]{2,0,1:T(8,128)(2,1)}, bf16[96,3,262]{2,0,1:T(8,128)(2,1)S(1)}, u32[]{:S(2)}, u32[]{:S(2)}) collective-permute-start(bf16[96,3,262]{2,0,1:T(8,128)(2,1)} %collective-permute-done.9), channel_id=1, source_target_pairs={{0,32},{32,0},{16,48},{48,16},{64,96},{96,64},{80,112},{112,80},{1... | collective-permute-start | bytes 452744 | tf_op jit(solution)/shard_map/ppermute | solution.py:14
  143.5 412.4 %all-reduce.10.cloned.1.call-start = ((), (), s32[]{:S(2)}) async-start(), calls=%async_computation.1 | async-start | bytes 393216 | tf_op jit(solution)/shard_map/psum | solution.py:137
  313.4 17.1 %collective-permute-start.11 = (bf16[96,3,262]{2,0,1:T(8,128)(2,1)S(1)}, bf16[96,3,262]{2,0,1:T(8,128)(2,1)S(1)}, u32[]{:S(2)}, u32[]{:S(2)}) collective-permute-start(bf16[96,3,262]{2,0,1:T(8,128)(2,1)S(1)} %collective-permute-done.10), channel_id=1, source_target_pairs={{0,64},{64,0},{16,80},{80,16},{32,96},{96,32},{48,112},{112,48},{1... | collective-permute-start | bytes 452744 | tf_op jit(solution)/shard_map/ppermute | solution.py:14
  330.5 17.7 %collective-permute-start.12 = (bf16[96,3,262]{2,0,1:T(8,128)(2,1)S(1)}, bf16[96,3,262]{2,0,1:T(8,128)(2,1)S(1)}, u32[]{:S(2)}, u32[]{:S(2)}) collective-permute-start(bf16[96,3,262]{2,0,1:T(8,128)(2,1)S(1)} %collective-permute-done.11), channel_id=1, source_target_pairs={{0,128},{128,0},{16,144},{144,16},{32,160},{160,32},{48,176},{176,... | collective-permute-start | bytes 452744 | tf_op jit(solution)/shard_map/ppermute | solution.py:14
  348.2 65.4 %collective-permute-start.13 = (bf16[96,3,262]{2,0,1:T(8,128)(2,1)S(1)}, bf16[96,3,262]{2,0,1:T(8,128)(2,1)S(1)}, u32[]{:S(2)}, u32[]{:S(2)}) collective-permute-start(bf16[96,3,262]{2,0,1:T(8,128)(2,1)S(1)} %collective-permute-done.12), channel_id=1, source_target_pairs={{0,256},{256,0},{16,272},{272,16},{32,288},{288,32},{48,304},{304,... | collective-permute-start | bytes 452744 | tf_op jit(solution)/shard_map/ppermute | solution.py:14
  415.5 142.0 %collective-permute-start.14 = (bf16[96,3,262]{2,0,1:T(8,128)(2,1)S(1)}, bf16[96,3,262]{2,0,1:T(8,128)(2,1)}, u32[]{:S(2)}, u32[]{:S(2)}) collective-permute-start(bf16[96,3,262]{2,0,1:T(8,128)(2,1)S(1)} %get-tuple-element.167), channel_id=1, source_target_pairs={{0,1},{1,2},{2,3},{3,4},{4,5},{5,6},{6,7},{7,8},{8,9},{9,10},{10,1... | collective-permute-start | bytes 452744 | tf_op jit(solution)/shard_map/ppermute | solution.py:24
  418.6 139.0 %collective-permute-start.15 = (bf16[96,3,262]{2,0,1:T(8,128)(2,1)}, bf16[96,3,262]{2,0,1:T(8,128)(2,1)}, u32[]{:S(2)}, u32[]{:S(2)}) collective-permute-start(bf16[96,3,262]{2,0,1:T(8,128)(2,1)} %get-tuple-element.168), channel_id=1, source_target_pairs={{1,0},{2,1},{3,2},{4,3},{5,4},{6,5},{7,6},{8,7},{9,8},{10,9},{11,1... | collective-permute-start | bytes 452744 | tf_op jit(solution)/shard_map/ppermute | solution.py:25
  560.4 18.9 %collective-permute-start.16 = (f32[3,768]{1,0:T(4,128)S(1)}, f32[3,768]{1,0:T(4,128)S(1)}, u32[]{:S(2)}, u32[]{:S(2)}) collective-permute-start(f32[3,768]{1,0:T(4,128)S(1)} %slice.926), channel_id=1, source_target_pairs={{0,16},{16,32},{32,48},{48,64},{64,80},{80,96},{96,112},{112,128},... | collective-permute-start | bytes 27656 | tf_op jit(solution)/shard_map/ppermute | solution.py:24
  577.4 8.0 %collective-permute-start.17 = (f32[3,768]{1,0:T(4,128)S(1)}, f32[3,768]{1,0:T(4,128)S(1)}, u32[]{:S(2)}, u32[]{:S(2)}) collective-permute-start(f32[3,768]{1,0:T(4,128)S(1)} %slice.929), channel_id=1, source_target_pairs={{16,0},{32,16},{48,32},{64,48},{80,64},{96,80},{112,96},{128,112},... | collective-permute-start | bytes 27656 | tf_op jit(solution)/shard_map/ppermute | solution.py:25
  (95 other events, 1800.6 us)
Sparse Core Ops, SparseCore 0:
  143.6 269.9 all-reduce.7
  416.8 139.0 all-reduce.9
